TPU v7x, 256 devices: a whole 4x4x8 slice. The times are simulated.
256 devices in a mesh: section: 2 (over x_lo), group: 4 (over x_hi, core), mp: 32 (over y, z).
Axes of the slice: x: 4 (x_hi: 2, x_lo: 2; x = x_hi * 2 + x_lo), y: 4, z: 8, core: 2. Of those that a mesh axis runs over, the one named last changes fastest.
Arguments:
- hidden: bfloat16 [2, 3072, 28672], P('section', 'group', 'mp'), may hold values from -6 to 6
- down_weight: bfloat16 [2, 28672, 8192], P('section', 'mp', 'group'), may hold values from -0.0625 to 0.0625
- residual: bfloat16 [2, 3072, 8192], P('section', ('group', 'mp')), may hold values from -12 to 12
- norm_gain: float32 [2, 8192], P('section', 'mp'), may hold values from 0.25 to 1.75
Outputs:
- handed: bfloat16 [2, 3072, 8192], P('section', 'group', 'mp')
- normed: bfloat16 [2, 3072, 8192], P('section', 'group', 'mp')
All inputs are finite; a program needn't handle non-finite values.
Results may differ from a plain program's by a relative error of at most 0.017.
Values may be sent and summed in bfloat16 or wider, within the bound.
No kernel may reach another device: no remote copies, remote signals or barrier semaphores. Data moves between devices by JAX's collectives and lax.ppermute only.
A program may use at most 128 MiB of HBM per device.

v0:
```python
import jax
import jax.numpy as jnp
from jax import lax
from jax.sharding import PartitionSpec as P

D = 8192


def passed_along(x, axis, by):
    length = lax.axis_size(axis)
    return lax.ppermute(x, axis, [(i, (i + by) % length) for i in range(length)])


def shards(hidden, down_weight, residual, norm_gain):
    local_hidden = hidden[0]
    local_weight = down_weight[0]
    term = jnp.dot(
        local_hidden,
        lax.all_gather(local_weight, "group", axis=1, tiled=True),
        preferred_element_type=jnp.float32,
    )
    summed = lax.psum_scatter(
        term.astype(jnp.bfloat16), "mp", scatter_dimension=0, tiled=True
    ).astype(jnp.float32)
    stream = (residual[0].astype(jnp.float32) + summed).astype(jnp.bfloat16)
    regrouped = lax.all_to_all(stream, "mp", split_axis=1, concat_axis=0, tiled=True)
    handed = passed_along(regrouped, "section", 1)
    values = handed.astype(jnp.float32)
    squares = lax.psum(jnp.sum(values * values, axis=1), "mp")
    scale = lax.rsqrt(squares / D + 1e-05)
    normed = (values * scale[:, None] * norm_gain[0][None, :]).astype(jnp.bfloat16)
    return (handed[None], normed[None])


def solution(mesh):
    placed = (
        P("section", "group", "mp"),
        P("section", "mp", "group"),
        P("section", ("group", "mp"), None),
        P("section", "mp"),
    )
    return jax.shard_map(
        shards,
        mesh=mesh,
        in_specs=placed,
        out_specs=(P("section", "group", "mp"), P("section", "group", "mp")),
        check_vma=False,
    )
```

profile of v0, /device:TPU:2, one launch (start us, length us, event | category | flops | bytes accessed | tf_op | source)
XLA Modules:
  0.0 479.8 jit_solution(16720687751090415899)
XLA Ops:
  7.2 0.0 copy-start
  7.2 0.0 all-gather.3.cloned.1.call-start
  7.2 0.7 all-gather.3.cloned.1.call-update
  7.9 0.0 reduce-scatter.2.cloned.1.call-start
  8.0 104.6 %all-gather.3.cloned.1.call-done = bf16[1,896,8192]{2,1,0:T(8,128)(2,1)} async-done(((bf16[1,896,2048]{2,1,0:T(8,128)(2,1)}), bf16[1,896,8192]{2,1,0:T(8,128)(2,1)}) %all-gather.3.cloned.1.call-update) | async-done | bytes 14680080 | tf_op jit(solution)/shard_map/all_gather | solution.py:19
  112.5 0.0 copy-done
  112.5 20.6 %fusion.2 = bf16[768,8192]{1,0:T(8,128)(2,1)} fusion(bf16[1,896,8192]{2,1,0:T(8,128)(2,1)} %all-gather.3.cloned.1.call-done, bf16[1,768,896]{2,1,0:T(8,128)(2,1)S(1)} %copy-done), kind=kOutput, calls=%fused_computation.2 | convolution fusion | flops 11280580608 | bytes 28639232 | tf_op jit(solution)/shard_map/dot_general | solution.py:17
  133.2 0.0 copy-start.1
  133.2 0.0 copy-start.2
  133.2 0.0 reduce-scatter.2.cloned.1.call-update
  133.2 238.1 %reduce-scatter.2.cloned.1.call-done = bf16[24,8192]{1,0:T(8,128)(2,1)} async-done(((bf16[768,8192]{1,0:T(8,128)(2,1)}), bf16[24,8192]{1,0:T(8,128)(2,1)}) %reduce-scatter.2.cloned.1.call-update) | async-done | bytes 393232 | tf_op jit(solution)/shard_map/reduce_scatter | solution.py:22
  371.3 0.0 copy-done.1
  371.3 1.1 fusion.9
  372.5 18.4 %all_to_all.19 = bf16[24,32,256]{2,0,1:T(8,128)(2,1)S(1)} all-to-all(bf16[24,32,256]{2,0,1:T(8,128)(2,1)S(1)} %bitcast.23), channel_id=1, replica_groups=mesh['section'=2,'group'=4,'mp'=32] {'mp'}, dimensions={1} | all-to-all | bytes 786432 | tf_op jit(solution)/shard_map/all_to_all | solution.py:26
  390.9 0.6 collective-permute-start
  391.4 7.2 %collective-permute-done = bf16[768,256]{1,0:T(8,128)(2,1)S(1)} collective-permute-done((bf16[768,256]{1,0:T(8,128)(2,1)S(1)}, bf16[768,256]{1,0:T(8,128)(2,1)S(1)}, u32[]{:S(2)}, u32[]{:S(2)}) %collective-permute-start) | collective-permute-done | bytes 393248 | tf_op jit(solution)/shard_map/ppermute | solution.py:11
  398.7 0.2 fusion.6
  398.8 72.5 %psum.7 = f32[768]{0:T(1024)S(1)} all-reduce(f32[768]{0:T(1024)S(1)} %fusion.6), channel_id=1, replica_groups=mesh['section'=2,'group'=4,'mp'=32] {'mp'}, use_global_device_ids=true, to_apply=%region_2.0 | all-reduce | flops 768 | bytes 6144 | tf_op jit(solution)/shard_map/psum | solution.py:29
  471.3 0.0 copy-done.2
  471.3 0.9 fusion.10
  472.3 0.7 copy.12
  (2 shorter events, 0.0 us)
Async XLA Ops:
  7.2 105.3 %copy-start = (bf16[1,768,896]{2,1,0:T(8,128)(2,1)S(1)}, bf16[1,768,896]{2,1,0:T(8,128)(2,1)}, u32[]{:S(2)}) copy-start(bf16[1,768,896]{2,1,0:T(8,128)(2,1)} %param.4) | copy-start | bytes 4128772
  7.2 105.3 %all-gather.3.cloned.1.call-start = ((), (), s32[]{:S(2)}) async-start(), calls=%async_computation.3 | async-start | bytes 18350080 | tf_op jit(solution)/shard_map/all_gather | solution.py:19
  7.9 363.4 %reduce-scatter.2.cloned.1.call-start = ((), (), s32[]{:S(2)}) async-start(), calls=%async_computation.2 | async-start | bytes 12976128 | tf_op jit(solution)/shard_map/reduce_scatter | solution.py:22
  133.2 238.2 %copy-start.1 = (bf16[1,24,8192]{2,1,0:T(8,128)(2,1)S(1)}, bf16[1,24,8192]{2,1,0:T(8,128)(2,1)}, u32[]{:S(2)}) copy-start(bf16[1,24,8192]{2,1,0:T(8,128)(2,1)} %param.6) | copy-start | bytes 1179652
  133.2 338.2 %copy-start.2 = (f32[1,256]{1,0:T(1,128)S(1)}, f32[1,256]{1,0:T(1,128)}, u32[]{:S(2)}) copy-start(f32[1,256]{1,0:T(1,128)} %param.7) | copy-start | bytes 3076
  390.9 7.8 %collective-permute-start = (bf16[768,256]{1,0:T(8,128)(2,1)S(1)}, bf16[768,256]{1,0:T(8,128)(2,1)S(1)}, u32[]{:S(2)}, u32[]{:S(2)}) collective-permute-start(bf16[768,256]{1,0:T(8,128)(2,1)S(1)} %bitcast.25), channel_id=1, source_target_pairs={{0,128},{128,0},{1,129},{129,1},{2,130},{130,2},{3,131},{131,3},{4... | collective-permute-start | bytes 1179656 | tf_op jit(solution)/shard_map/ppermute | solution.py:11
Sparse Core Ops, SparseCore 0:
  9.8 102.6 all-gather.2
  133.3 237.9 reduce-scatter.1
where the time goes:
time: 480 us
  waiting for transfers between devices  351 us (73%)
  blocking collectives  90.9 us (19%)
  matrix products  20.6 us (4%)
  between operations  14.1 us (3%)
    reduce_scatter x1, waiting for transfers between devices, shards(): lax.psum_scatter(term.astype(jnp.bfloat16), 'mp', scatter_dimension=0, ti...  238 us
    all_gather x1, waiting for transfers between devices, shards(): lax.all_gather(local_weight, 'group', axis=1, tiled=True)  105 us
    psum x1, blocking collectives, shards(): squares = lax.psum(jnp.sum(values * values, axis=1), 'mp')  72.5 us
    dot_general x1, matrix products, shards(): jnp.dot(local_hidden, lax.all_gather(local_weight, 'group', axis=1, tiled...  20.6 us
    all_to_all x1, blocking collectives, shards(): lax.all_to_all(stream, 'mp', split_axis=1, concat_axis=0, tiled=True)  18.4 us
  transfers between devices with their start and end apart: 3, of which 3 were waited for; matrix products, arithmetic and copies ran while one was open for 0% of the time, Pallas kernels for 0%

commit v1 on v0

--- a/solution.py
+++ b/solution.py
@@ -26,7 +26,7 @@
     regrouped = lax.all_to_all(stream, "mp", split_axis=1, concat_axis=0, tiled=True)
     handed = passed_along(regrouped, "section", 1)
     values = handed.astype(jnp.float32)
-    squares = lax.psum(jnp.sum(values * values, axis=1), "mp")
+    squares = jnp.sum(lax.all_gather(jnp.sum(values * values, axis=1), "mp"), axis=0)
     scale = lax.rsqrt(squares / D + 1e-05)
     normed = (values * scale[:, None] * norm_gain[0][None, :]).astype(jnp.bfloat16)
     return (handed[None], normed[None])

time: 480 us -> 450 us (0.938)
  blocking collectives: 90.9 us -> 61.1 us
    psum x1 -> x0, blocking collectives: 72.5 us -> none  [shards(): squares = lax.psum(jnp.sum(values * values, axis=1), 'mp')]
    all_gather x0 -> x1, blocking collectives: none -> 42.7 us  [shards(): lax.all_gather(jnp.sum(values * values, axis=1), 'mp')]
where the time goes in v1:
time: 450 us
  waiting for transfers between devices  351 us (78%)
  blocking collectives  61.1 us (14%)
  matrix products  20.6 us (5%)
  between operations  14.1 us (3%)
    reduce_scatter x1, waiting for transfers between devices, shards(): lax.psum_scatter(term.astype(jnp.bfloat16), 'mp', scatter_dimension=0, ti...  238 us
    all_gather x1, waiting for transfers between devices, shards(): lax.all_gather(local_weight, 'group', axis=1, tiled=True)  105 us
    all_gather x1, blocking collectives, shards(): lax.all_gather(jnp.sum(values * values, axis=1), 'mp')  42.7 us
    dot_general x1, matrix products, shards(): jnp.dot(local_hidden, lax.all_gather(local_weight, 'group', axis=1, tiled...  20.6 us
    all_to_all x1, blocking collectives, shards(): lax.all_to_all(stream, 'mp', split_axis=1, concat_axis=0, tiled=True)  18.4 us
  transfers between devices with their start and end apart: 3, of which 3 were waited for; matrix products, arithmetic and copies ran while one was open for 0% of the time, Pallas kernels for 0%

profile of v1, /device:TPU:2, one launch (start us, length us, event | category | flops | bytes accessed | tf_op | source)
XLA Modules:
  0.0 450.2 jit_solution(7978087672557653465)
XLA Ops:
  7.2 0.0 copy-start
  7.2 0.0 all-gather.5.cloned.1.call-start
  7.2 0.7 all-gather.5.cloned.1.call-update
  7.9 0.0 reduce-scatter.2.cloned.1.call-start
  8.0 104.6 %all-gather.5.cloned.1.call-done = bf16[1,896,8192]{2,1,0:T(8,128)(2,1)} async-done(((bf16[1,896,2048]{2,1,0:T(8,128)(2,1)}), bf16[1,896,8192]{2,1,0:T(8,128)(2,1)}) %all-gather.5.cloned.1.call-update) | async-done | bytes 14680080 | tf_op jit(solution)/shard_map/all_gather | solution.py:19
  112.5 0.0 copy-done
  112.5 20.6 %fusion.2 = bf16[768,8192]{1,0:T(8,128)(2,1)} fusion(bf16[1,896,8192]{2,1,0:T(8,128)(2,1)} %all-gather.5.cloned.1.call-done, bf16[1,768,896]{2,1,0:T(8,128)(2,1)S(1)} %copy-done), kind=kOutput, calls=%fused_computation.2 | convolution fusion | flops 11280580608 | bytes 28639232 | tf_op jit(solution)/shard_map/dot_general | solution.py:17
  133.2 0.0 copy-start.1
  133.2 0.0 copy-start.2
  133.2 0.0 reduce-scatter.2.cloned.1.call-update
  133.2 238.1 %reduce-scatter.2.cloned.1.call-done = bf16[24,8192]{1,0:T(8,128)(2,1)} async-done(((bf16[768,8192]{1,0:T(8,128)(2,1)}), bf16[24,8192]{1,0:T(8,128)(2,1)}) %reduce-scatter.2.cloned.1.call-update) | async-done | bytes 393232 | tf_op jit(solution)/shard_map/reduce_scatter | solution.py:22
  371.3 0.0 copy-done.1
  371.3 1.1 fusion.9
  372.5 18.4 %all_to_all.19 = bf16[24,32,256]{2,0,1:T(8,128)(2,1)S(1)} all-to-all(bf16[24,32,256]{2,0,1:T(8,128)(2,1)S(1)} %bitcast.23), channel_id=1, replica_groups=mesh['section'=2,'group'=4,'mp'=32] {'mp'}, dimensions={1} | all-to-all | bytes 786432 | tf_op jit(solution)/shard_map/all_to_all | solution.py:26
  390.9 0.6 collective-permute-start
  391.4 7.2 %collective-permute-done = bf16[768,256]{1,0:T(8,128)(2,1)S(1)} collective-permute-done((bf16[768,256]{1,0:T(8,128)(2,1)S(1)}, bf16[768,256]{1,0:T(8,128)(2,1)S(1)}, u32[]{:S(2)}, u32[]{:S(2)}) %collective-permute-start) | collective-permute-done | bytes 393248 | tf_op jit(solution)/shard_map/ppermute | solution.py:11
  398.7 0.2 fusion.6
  398.9 42.7 %all-gather.2 = f32[32,1,768]{2,1,0:T(1,128)S(1)} all-gather(f32[1,1,768]{2,1,0:T(1,128)S(1)} %reshape.17), channel_id=3, replica_groups=mesh['section'=2,'group'=4,'mp'=32] {'mp'}, dimensions={0}, use_global_device_ids=true | all-gather | bytes 101376 | tf_op jit(solution)/shard_map/all_gather | solution.py:29
  441.6 0.1 reduce_sum.19
  441.6 0.0 copy-done.2
  441.7 0.9 fusion.10
  442.6 0.7 copy.12
  (3 shorter events, 0.0 us)
Async XLA Ops:
  7.2 105.3 %copy-start = (bf16[1,768,896]{2,1,0:T(8,128)(2,1)S(1)}, bf16[1,768,896]{2,1,0:T(8,128)(2,1)}, u32[]{:S(2)}) copy-start(bf16[1,768,896]{2,1,0:T(8,128)(2,1)} %param.4) | copy-start | bytes 4128772
  7.2 105.3 %all-gather.5.cloned.1.call-start = ((), (), s32[]{:S(2)}) async-start(), calls=%async_computation.3 | async-start | bytes 18350080 | tf_op jit(solution)/shard_map/all_gather | solution.py:19
  7.9 363.4 %reduce-scatter.2.cloned.1.call-start = ((), (), s32[]{:S(2)}) async-start(), calls=%async_computation.2 | async-start | bytes 12976128 | tf_op jit(solution)/shard_map/reduce_scatter | solution.py:22
  133.2 238.2 %copy-start.1 = (bf16[1,24,8192]{2,1,0:T(8,128)(2,1)S(1)}, bf16[1,24,8192]{2,1,0:T(8,128)(2,1)}, u32[]{:S(2)}) copy-start(bf16[1,24,8192]{2,1,0:T(8,128)(2,1)} %param.6) | copy-start | bytes 1179652
  133.2 308.5 %copy-start.2 = (f32[1,256]{1,0:T(1,128)S(1)}, f32[1,256]{1,0:T(1,128)}, u32[]{:S(2)}) copy-start(f32[1,256]{1,0:T(1,128)} %param.7) | copy-start | bytes 3076
  390.9 7.8 %collective-permute-start = (bf16[768,256]{1,0:T(8,128)(2,1)S(1)}, bf16[768,256]{1,0:T(8,128)(2,1)S(1)}, u32[]{:S(2)}, u32[]{:S(2)}) collective-permute-start(bf16[768,256]{1,0:T(8,128)(2,1)S(1)} %bitcast.25), channel_id=1, source_target_pairs={{0,128},{128,0},{1,129},{129,1},{2,130},{130,2},{3,131},{131,3},{4... | collective-permute-start | bytes 1179656 | tf_op jit(solution)/shard_map/ppermute | solution.py:11
Sparse Core Ops, SparseCore 0:
  9.8 102.6 all-gather.4
  133.3 237.9 reduce-scatter.1
